TPU v7x, 32 devices: a whole 2x2x4 slice. The times are simulated.
32 devices in a mesh: ind: 8 (over z, core), snp: 4 (over y, x).
Axes of the slice: x: 2, y: 2, z: 4, core: 2. Of those that a mesh axis runs over, the one named last changes fastest.
Arguments:
- dosages: int32 [2048, 2048], P(('snp', 'ind')), may hold values from 0 to 2
- allele_freq: float32 [2048], P(('snp', 'ind')), may hold values from 0.05 to 0.5
- earlier_factor: bfloat16 [2048, 8192], P(None, 'ind'), may hold values from -0.09375 to 0.09375
- earlier_solved: bfloat16 [8192, 2048], P('ind', 'snp'), may hold values from -6 to 6
- diag_inverse: bfloat16 [2048, 512], P('ind'), as said below
- update_products: bfloat16 [2048, 2048], P('ind'), may hold values from -0.125 to 0.125
Outputs:
- whitened: bfloat16 [2048, 2048], P('ind', 'snp')
Inputs may be any that keep to these rules, and one draw needn't show every extreme that they name: `diag_inverse`: within each block of 512 rows the entry in row r and column c is zero where c > r mod 512; the entries with c = r mod 512 lie in 0.6 to 1.4.
All inputs are finite; a program needn't handle non-finite values.
Results may differ from a plain program's by a relative error of at most 0.0058.
Values may be sent and summed in bfloat16 or wider, within the bound.
A program may use at most 64 MiB of HBM per device.

v0:
```python
import jax
import jax.numpy as jnp
from jax import lax
from jax.sharding import PartitionSpec as P

SLAB = 2048
BLK = 512


def partner_2(value, axis, stride):
    mask = 2**stride
    pairs = [(source, source ^ mask) for source in range(lax.axis_size(axis))]
    return lax.ppermute(value, axis, pairs)


def per_device(dosages, allele_freq, earlier_factor, earlier_solved, diag_inverse, update_products):
    frequency = allele_freq[:, None]
    scaled = (
        (dosages.astype(jnp.float32) - 2.0 * frequency)
        * lax.rsqrt(2.0 * frequency * (1.0 - frequency))
    ).astype(jnp.bfloat16)
    arrived = lax.all_to_all(scaled, "ind", split_axis=1, concat_axis=0, tiled=True)
    standardized = arrived.T
    rows_dev = diag_inverse.shape[0]
    snp_width = earlier_solved.shape[1]
    update = lax.psum_scatter(
        jnp.dot(earlier_factor, earlier_solved, preferred_element_type=jnp.float32),
        "ind",
        scatter_dimension=0,
        tiled=True,
    )
    residual = (standardized.astype(jnp.float32) - update).astype(jnp.bfloat16)
    position = lax.axis_index("ind")
    my_start = position * rows_dev
    my_block = my_start // BLK
    owners = BLK // rows_dev
    held = residual
    for bit in range(owners.bit_length() - 1):
        partner = partner_2(held, "ind", bit)
        lower_side = position // 2**bit % 2 == 0
        held = jnp.where(
            lower_side, jnp.concatenate((held, partner), 0), jnp.concatenate((partner, held), 0)
        )
    diagonal_term = jnp.dot(diag_inverse, held, preferred_element_type=jnp.float32)
    solved = jnp.where(
        my_block == 0,
        diagonal_term.astype(jnp.bfloat16),
        jnp.zeros((rows_dev, snp_width), jnp.bfloat16),
    )
    blocks = SLAB // BLK
    for block in range(1, blocks):
        carried = jnp.dot(
            update_products,
            lax.all_gather(solved, "ind", axis=0, tiled=True),
            preferred_element_type=jnp.float32,
        )
        solved = jnp.where(
            my_block == block, (diagonal_term - carried).astype(jnp.bfloat16), solved
        )
    return solved


def solution(mesh):
    placed = (
        P(("snp", "ind"), None),
        P(("snp", "ind")),
        P(None, "ind"),
        P("ind", "snp"),
        P("ind", None),
        P("ind", None),
    )
    return jax.shard_map(
        per_device, mesh=mesh, in_specs=placed, out_specs=P("ind", "snp"), check_vma=False
    )
```

profile of v0, /device:TPU:9, one launch (start us, length us, event | category | flops | bytes accessed | tf_op | source)
XLA Modules:
  0.0 181.5 jit_solution(13819635781479576580)
XLA Ops:
  6.5 0.0 copy-start
  6.5 0.0 reduce-scatter.2.cloned.1.call-start
  6.5 1.2 copy-done
  7.8 6.5 %fusion.18 = f32[2048,512]{1,0:T(8,128)} fusion(bf16[2048,1024]{1,0:T(8,128)(2,1)} %param.8, bf16[1024,512]{1,0:T(8,128)(2,1)S(1)} %copy-done), kind=kOutput, calls=%fused_computation.28 | convolution fusion | flops 2147483648 | bytes 9437184 | tf_op jit(solution)/shard_map/dot_general | solution.py:27
  14.3 0.0 reduce-scatter.2.cloned.1.call-update
  14.3 0.0 all-gather.4.cloned.1.call-start
  14.3 0.6 copy-done.4
  14.9 0.4 copy-done.1
  15.3 0.1 multiply_convert_fusion
  15.5 0.0 copy-start.3
  15.5 17.0 %all_to_all.13 = bf16[64,8,256]{2,0,1:T(8,128)(2,1)S(1)} all-to-all(bf16[64,8,256]{2,0,1:T(8,128)(2,1)S(1)} %bitcast.38), channel_id=1, replica_groups=mesh['ind'=8,'snp'=4] {'ind'}, dimensions={1} | all-to-all | bytes 524288 | tf_op jit(solution)/shard_map/all_to_all | solution.py:22
  32.5 0.2 copy.15
  32.7 36.7 %reduce-scatter.2.cloned.1.call-done = f32[256,512]{1,0:T(8,128)} async-done(((f32[2048,512]{1,0:T(8,128)}), f32[256,512]{1,0:T(8,128)}) %reduce-scatter.2.cloned.1.call-update) | async-done | bytes 524304 | tf_op jit(solution)/shard_map/reduce_scatter | solution.py:26
  69.4 1.1 fusion.15
  70.5 0.0 copy-start.2
  70.6 0.1 collective-permute-start
  70.7 1.5 collective-permute-done
  72.2 0.4 fusion.9
  72.5 0.7 select_bitcast_fusion
  73.3 0.0 all-gather.4.cloned.1.call-update
  73.3 0.0 all-gather.6.cloned.1.call-start
  73.3 32.1 %all-gather.4.cloned.1.call-done = bf16[2048,512]{0,1:T(8,128)(2,1)} async-done(((bf16[256,512]{0,1:T(8,128)(2,1)}), bf16[2048,512]{0,1:T(8,128)(2,1)}) %all-gather.4.cloned.1.call-update) | async-done | bytes 2097168 | tf_op jit(solution)/shard_map/all_gather | solution.py:54
  105.5 0.0 copy-done.2
  105.5 3.0 %fusion.8 = bf16[256,512]{0,1:T(8,128)(2,1)} fusion(f32[512,256]{1,0:T(8,128)S(1)} %fusion.9, bf16[2048,512]{0,1:T(8,128)(2,1)} %all-gather.4.cloned.1.call-done, bf16[256,2048]{1,0:T(8,128)(2,1)S(1)} %copy-done.2, pred[]{:T(512)S(6)} %eq.20, pred[]{:T(512)S(6)} %eq.21), kind=kOutput, calls=%fused_computation.11 | convolution fusion | flops 537526272 | bytes 3932162 | tf_op jit(solution)/shard_map/dot_general | solution.py:52
  108.5 0.0 all-gather.6.cloned.1.call-update
  108.6 0.0 all-gather.8.cloned.1.call-start
  108.6 30.0 %all-gather.6.cloned.1.call-done = bf16[2048,512]{0,1:T(8,128)(2,1)} async-done(((bf16[256,512]{0,1:T(8,128)(2,1)}), bf16[2048,512]{0,1:T(8,128)(2,1)}) %all-gather.6.cloned.1.call-update) | async-done | bytes 2097168 | tf_op jit(solution)/shard_map/all_gather | solution.py:54
  138.6 3.0 %fusion.6 = bf16[256,512]{0,1:T(8,128)(2,1)} fusion(bf16[256,512]{0,1:T(8,128)(2,1)} %fusion.8, f32[512,256]{1,0:T(8,128)S(1)} %fusion.9, bf16[2048,512]{0,1:T(8,128)(2,1)} %all-gather.6.cloned.1.call-done, bf16[256,2048]{1,0:T(8,128)(2,1)S(1)} %copy-done.2, pred[]{:T(512)S(6)} %eq.19), kind=kOutput, calls=%fused_computation.9 | convolution fusion | flops 537264128 | bytes 4194305 | tf_op jit(solution)/shard_map/dot_general | solution.py:52
  141.7 0.0 all-gather.8.cloned.1.call-update
  141.7 30.1 %all-gather.8.cloned.1.call-done = bf16[2048,512]{0,1:T(8,128)(2,1)} async-done(((bf16[256,512]{0,1:T(8,128)(2,1)}), bf16[2048,512]{0,1:T(8,128)(2,1)}) %all-gather.8.cloned.1.call-update) | async-done | bytes 2097168 | tf_op jit(solution)/shard_map/all_gather | solution.py:54
  171.7 2.3 %fusion.4 = bf16[256,512]{0,1:T(8,128)(2,1)S(1)} fusion(bf16[256,512]{0,1:T(8,128)(2,1)} %fusion.6, f32[512,256]{1,0:T(8,128)S(1)} %fusion.9, bf16[2048,512]{0,1:T(8,128)(2,1)} %all-gather.8.cloned.1.call-done, bf16[256,2048]{1,0:T(8,128)(2,1)S(1)} %copy-done.2, pred[]{:T(512)S(6)} %eq.17), kind=kOutput, calls=%fused_computation.7 | convolution fusion | flops 537264128 | bytes 4194305 | tf_op jit(solution)/shard_map/dot_general | solution.py:52
  174.1 0.8 copy.16
  (6 shorter events, 0.1 us)
Async XLA Ops:
  6.5 1.2 copy-start
  6.5 62.9 %reduce-scatter.2.cloned.1.call-start = ((), (), s32[]{:S(2)}) async-start(), calls=%async_computation.2 | async-start | bytes 4718592 | tf_op jit(solution)/shard_map/reduce_scatter | solution.py:26
  14.3 0.7 copy-start.4
  14.3 1.1 copy-start.1
  14.3 91.2 %all-gather.4.cloned.1.call-start = ((), (), s32[]{:S(2)}) async-start(), calls=%async_computation.3 | async-start | bytes 2359296 | tf_op jit(solution)/shard_map/all_gather | solution.py:54
  15.5 56.7 %copy-start.3 = (bf16[256,512]{1,0:T(8,128)(2,1)S(1)}, bf16[256,512]{1,0:T(8,128)(2,1)}, u32[]{:S(2)}) copy-start(bf16[256,512]{1,0:T(8,128)(2,1)} %param.10) | copy-start | bytes 786436
  70.5 34.9 %copy-start.2 = (bf16[256,2048]{1,0:T(8,128)(2,1)S(1)}, bf16[256,2048]{1,0:T(8,128)(2,1)}, u32[]{:S(2)}) copy-start(bf16[256,2048]{1,0:T(8,128)(2,1)} %param.11) | copy-start | bytes 3145732
  70.6 1.6 collective-permute-start
  73.3 65.3 %all-gather.6.cloned.1.call-start = ((), (), s32[]{:S(2)}) async-start(), calls=%async_computation.4 | async-start | bytes 2359296 | tf_op jit(solution)/shard_map/all_gather | solution.py:54
  108.6 63.2 %all-gather.8.cloned.1.call-start = ((), (), s32[]{:S(2)}) async-start(), calls=%async_computation.5 | async-start | bytes 2359296 | tf_op jit(solution)/shard_map/all_gather | solution.py:54
Sparse Core Ops, SparseCore 0:
  14.4 54.9 reduce-scatter.1
  73.4 32.0 all-gather.3
  108.7 29.8 all-gather.5
  141.8 29.8 all-gather.7
where the time goes:
time: 182 us; the launch traced here: 181 us
  waiting for transfers between devices  130 us (71%)
  blocking collectives  17 us (9%)
  matrix products  15.3 us (8%)
  between operations  13.2 us (7%)
  local copies, waits for them, and re-layouts  3.27 us (2%)
  other arithmetic  2.03 us (1%)
    all_gather x3, waiting for transfers between devices, per_device(): lax.all_gather(solved, 'ind', axis=0, tiled=True)  92.2 us
    reduce_scatter x1, waiting for transfers between devices, per_device(): lax.psum_scatter(jnp.dot(earlier_factor, earlier_solved, preferred_elemen...  36.7 us
    all_to_all x1, blocking collectives, per_device(): lax.all_to_all(scaled, 'ind', split_axis=1, concat_axis=0, tiled=True)  17 us
    dot_general x3, matrix products, per_device(): jnp.dot(update_products, lax.all_gather(solved, 'ind', axis=0, tiled=True...  8.43 us
    dot_general x1, matrix products, per_device(): jnp.dot(earlier_factor, earlier_solved, preferred_element_type=jnp.float32)  6.49 us
  transfers between devices with their start and end apart: 5, of which 5 were waited for; matrix products, arithmetic and copies ran while one was open for 0% of the time, Pallas kernels for 0%

commit v1 on v0

v1 whole, which is shorter than its diff:
```python
import functools
import jax
import jax.numpy as jnp
from jax import lax
from jax.experimental import pallas as pl
from jax.experimental.pallas import tpu as pltpu
from jax.sharding import PartitionSpec as P

BLK = 512
CW = 128
BF = jnp.bfloat16
F32 = jnp.float32


def fused(chips, dos_h, freq_ref, a_h, b_h, d_h, u_h, out_ref,
          dos, a, b, dfull, ufull, scaled, acc, sib_out, sib_in,
          up_out, up_in, dn_out, dn_in, w,
          ld_sem, a_sem, x_sem, sib_s, sib_r, up_s, up_r, dn_s, dn_r, w_s, w_r, o_s, o_r):
    me = lax.axis_index("ind")
    z, c = me // 2, me % 2
    sib = z * 2 + 1 - c
    half = b_h.shape[1] // 2
    chunks = half // CW
    rows = d_h.shape[0]
    ucols = ufull.shape[1]
    snps = dos_h.shape[0]

    def remote(src, dst, ss, rs, to):
        return pltpu.make_async_remote_copy(
            src_ref=src, dst_ref=dst, send_sem=ss, recv_sem=rs,
            device_id={"ind": to}, device_id_type=pl.DeviceIdType.MESH)

    last = chips - 1

    def block_at(j):
        bottom = jnp.where(j < last - 1, j + 2, last - j)
        return jnp.where(z == 0, bottom, lax.rem(z + 1 + j, chips))

    def load_a(j):
        at = pl.ds(pl.multiple_of(block_at(j) * BLK, BLK), BLK)
        return pltpu.make_async_copy(a_h.at[at], a.at[at], a_sem.at[j])

    my_rows = pl.ds(pl.multiple_of(c * rows, rows), rows)
    load_dos = pltpu.make_async_copy(dos_h, dos, ld_sem.at[0])
    load_b = pltpu.make_async_copy(b_h, b, ld_sem.at[1])
    load_d = pltpu.make_async_copy(d_h, dfull.at[my_rows], ld_sem.at[2])
    load_u = pltpu.make_async_copy(u_h.at[:, :ucols], ufull.at[my_rows], ld_sem.at[3])
    load_dos.start()
    load_b.start()
    for j in range(chips):
        load_a(j).start()
    load_d.start()
    load_u.start()

    barrier = pltpu.get_barrier_semaphore()

    def greet(to):
        pl.semaphore_signal(barrier, inc=1, device_id={"ind": to},
                            device_id_type=pl.DeviceIdType.MESH)

    greet(sib)

    @pl.when(z > 0)
    def _():
        greet(me - 2)

    @pl.when(z < chips - 1)
    def _():
        greet(me + 2)

    load_dos.wait()
    frow = freq_ref[...]
    eye = (lax.broadcasted_iota(jnp.int32, (snps, snps), 0)
           == lax.broadcasted_iota(jnp.int32, (snps, snps), 1))
    freq = jnp.sum(jnp.where(eye, jnp.broadcast_to(frow, (snps, snps)), 0.0), axis=1, keepdims=True)
    scaled[...] = ((dos[...].astype(F32) - 2.0 * freq)
                   * lax.rsqrt(2.0 * freq * (1.0 - freq))).astype(BF)

    @pl.when((z == 0) | (z == chips - 1))
    def _():
        pl.semaphore_wait(barrier, 2)

    @pl.when((z > 0) & (z < chips - 1))
    def _():
        pl.semaphore_wait(barrier, 3)

    xd = remote(d_h, dfull.at[my_rows], x_sem.at[0], x_sem.at[1], sib)
    xu = remote(u_h.at[:, :ucols], ufull.at[my_rows], x_sem.at[2], x_sem.at[3], sib)

    def sib_copy(blk):
        return remote(sib_out.at[blk], sib_in.at[blk], sib_s.at[blk], sib_r.at[blk], sib)

    def up_copy(blk, q):
        return remote(up_out.at[blk, q], up_in.at[blk, q], up_s.at[blk, q], up_r.at[blk, q], me + 2)

    def dn_copy(blk, q):
        return remote(dn_out.at[blk, q], dn_in.at[blk, q], dn_s.at[blk, q], dn_r.at[blk, q], me - 2)

    def w_copy(blk, q):
        return remote(w.at[blk, q], w.at[blk, q], w_s.at[blk, q], w_r.at[blk, q], me + 2)

    def out_copy(q):
        return remote(
            w.at[z, q, pl.ds(pl.multiple_of((1 - c) * rows, rows), rows)],
            out_ref.at[:, pl.ds(pl.multiple_of(c * half + q * CW, CW), CW)],
            o_s.at[q], o_r.at[q], sib)

    def partial(blk, side):
        at = pl.ds(pl.multiple_of(blk * BLK, BLK), BLK)
        cols = pl.ds(pl.multiple_of(side * half, half), half)
        place = (lax.broadcasted_iota(jnp.int32, (snps, half), 1) + side * half
                 == lax.broadcasted_iota(jnp.int32, (snps, half), 0) + me * snps)
        own = lax.dot_general(scaled[:, at], place.astype(F32).astype(BF),
                              (((0,), (0,)), ((), ())), preferred_element_type=F32)
        return own - jnp.dot(a[at, :], b[:, cols], preferred_element_type=F32)

    def finish(blk):
        sib_copy(blk).wait_recv()
        for q in range(chunks):
            total = acc[blk, q] + sib_in[blk, :, q * CW:(q + 1) * CW].astype(F32)
            acc[blk, q] = total

            @pl.when((z == 0) & (blk > 0))
            def _():
                up_out[blk, q] = total.astype(BF)

            @pl.when((z == 0) & (blk > (1 if q else 0)))
            def _():
                up_copy(blk, q).start()

            @pl.when((z == chips - 1) & (blk < chips - 1))
            def _():
                dn_out[blk, q] = total.astype(BF)
                dn_copy(blk, q).start()

    load_b.wait()

    def step(j, carry):
        load_a(j).wait()
        blk = block_at(j)
        sib_out[blk] = partial(blk, 1 - c).astype(BF)
        sib_copy(blk).start()
        own = partial(blk, c)
        for q in range(chunks):
            acc[blk, q] = own[:, q * CW:(q + 1) * CW]

        @pl.when(j > 0)
        def _():
            finish(block_at(j - 1))

        return carry

    lax.fori_loop(0, chips, step, 0)
    xd.start()
    xu.start()
    finish(block_at(chips - 1))

    def role(zz):
        sent = []

        def send(copy):
            copy.start()
            sent.append(copy)

        def relay_up(blk, q):
            up_copy(blk, q).wait_recv()
            up_out[blk, q] = (acc[blk, q] + up_in[blk, q].astype(F32)).astype(BF)
            send(up_copy(blk, q))

        def relay_dn(blk, q):
            dn_copy(blk, q).wait_recv()
            dn_out[blk, q] = (acc[blk, q] + dn_in[blk, q].astype(F32)).astype(BF)
            send(dn_copy(blk, q))

        def residual(q):
            total = acc[zz, q]
            if zz < last:
                dn_copy(zz, q).wait_recv()
                total = total + dn_in[zz, q].astype(F32)
            if zz > 0:
                up_copy(zz, q).wait_recv()
                total = total + up_in[zz, q].astype(F32)
            acc[zz, q] = jnp.dot(dfull[...], total.astype(BF), preferred_element_type=F32)

        ready = []

        def weights():
            if not ready:
                load_d.wait()
                load_u.wait()
                xd.wait_recv()
                xu.wait_recv()
                ready.append(1)

        if 0 < zz < last:
            pieces = [(last - zz + k, q, 0, k) for k in range(zz) for q in range(chunks)]
            pieces += [(zz + k - 2, q, 1, k) for k in range(zz + 1, chips) for q in range(chunks)]
            for _, q, up, k in sorted(pieces):
                (relay_up if up else relay_dn)(k, q)
        weights()
        for q in range(chunks):
            residual(q)
            for k in range(zz):
                w_copy(k, q).wait_recv()
                if zz < last:
                    send(w_copy(k, q))
                acc[zz, q] = acc[zz, q] - jnp.dot(
                    ufull[:, k * BLK:(k + 1) * BLK], w[k, q], preferred_element_type=F32)
            finish_chunk(zz, q, send)
            if zz == 0 and q + 1 < chunks:
                up_copy(1, q + 1).start()
        for copy in sent:
            copy.wait_send()
        if zz == 0:
            for k in range(1, chips):
                for q in range(chunks):
                    up_copy(k, q).wait_send()
        if zz == last:
            for k in range(last):
                for q in range(chunks):
                    dn_copy(k, q).wait_send()

    def finish_chunk(zz, q, send):
        w[zz, q] = acc[zz, q].astype(BF)
        if zz < chips - 1:
            send(w_copy(zz, q))
        send(out_copy(q))
        out_ref[:, pl.ds(pl.multiple_of(c * half + q * CW, CW), CW)] = w[zz, q, my_rows, :]

    for zz in range(chips):
        pl.when(z == zz)(functools.partial(role, zz))

    for q in range(chunks):
        out_copy(q).wait_recv()
    for k in range(chips):
        sib_copy(k).wait_send()
    xd.wait_send()
    xu.wait_send()


def fused_call(dosages, allele_freq, earlier_factor, earlier_solved, diag_inverse, update_products):
    slab = earlier_factor.shape[0]
    chips = slab // BLK
    snps = dosages.shape[0]
    width = earlier_solved.shape[1]
    half = width // 2
    chunks = half // CW
    rows = diag_inverse.shape[0]
    depth = earlier_factor.shape[1]
    pieces = (chips, chunks, BLK, CW)
    dma = pltpu.SemaphoreType.DMA
    hbm = pl.BlockSpec(memory_space=pl.ANY)
    vmem = pl.BlockSpec(memory_space=pltpu.VMEM)
    macs = slab * depth * width + rows * (BLK + slab) * width
    return pl.pallas_call(
        functools.partial(fused, chips),
        out_shape=jax.ShapeDtypeStruct((rows, width), BF),
        in_specs=[hbm, vmem, hbm, hbm, hbm, hbm],
        out_specs=vmem,
        scratch_shapes=[
            pltpu.VMEM((snps, slab), jnp.int32),
            pltpu.VMEM((slab, depth), BF),
            pltpu.VMEM((depth, width), BF),
            pltpu.VMEM((BLK, BLK), BF),
            pltpu.VMEM((BLK, slab - BLK), BF),
            pltpu.VMEM((snps, slab), BF),
            pltpu.VMEM(pieces, F32),
            pltpu.VMEM((chips, BLK, half), BF),
            pltpu.VMEM((chips, BLK, half), BF),
            pltpu.VMEM(pieces, BF),
            pltpu.VMEM(pieces, BF),
            pltpu.VMEM(pieces, BF),
            pltpu.VMEM(pieces, BF),
            pltpu.VMEM(pieces, BF),
            dma((4,)), dma((chips,)), dma((4,)), dma((chips,)), dma((chips,)),
            dma((chips, chunks)), dma((chips, chunks)),
            dma((chips, chunks)), dma((chips, chunks)),
            dma((chips, chunks)), dma((chips, chunks)),
            dma((chunks,)), dma((chunks,)),
        ],
        compiler_params=pltpu.CompilerParams(
            collective_id=0, has_side_effects=True, vmem_limit_bytes=60 * 2**20),
        cost_estimate=pl.CostEstimate(
            flops=2 * macs, bytes_accessed=8 * 2**20, transcendentals=0),
    )(dosages, allele_freq.reshape(1, snps), earlier_factor, earlier_solved,
      diag_inverse, update_products)


def exchange_2(value, axis, stride):
    mask = 2**stride
    pairs = [(source, source ^ mask) for source in range(lax.axis_size(axis))]
    return lax.ppermute(value, axis, pairs)


def general(dosages, allele_freq, earlier_factor, earlier_solved, diag_inverse, update_products):
    slab = earlier_factor.shape[0]
    frequency = allele_freq[:, None]
    scaled = (
        (dosages.astype(F32) - 2.0 * frequency)
        * lax.rsqrt(2.0 * frequency * (1.0 - frequency))
    ).astype(BF)
    arrived = lax.all_to_all(scaled, "ind", split_axis=1, concat_axis=0, tiled=True)
    rows_dev = diag_inverse.shape[0]
    update = lax.psum_scatter(
        jnp.dot(earlier_factor, earlier_solved, preferred_element_type=F32),
        "ind", scatter_dimension=0, tiled=True)
    residual = (arrived.T.astype(F32) - update).astype(BF)
    position = lax.axis_index("ind")
    my_block = position * rows_dev // BLK
    held = residual
    for bit in range((BLK // rows_dev).bit_length() - 1):
        other = exchange_2(held, "ind", bit)
        held = jnp.where(
            position // 2**bit % 2 == 0,
            jnp.concatenate((held, other), 0), jnp.concatenate((other, held), 0))
    diagonal_term = jnp.dot(diag_inverse, held, preferred_element_type=F32)
    solved = jnp.where(my_block == 0, diagonal_term.astype(BF), jnp.zeros_like(residual))
    for block in range(1, slab // BLK):
        carried = jnp.dot(
            update_products, lax.all_gather(solved, "ind", axis=0, tiled=True),
            preferred_element_type=F32)
        solved = jnp.where(my_block == block, (diagonal_term - carried).astype(BF), solved)
    return solved


def solution(mesh):
    def per_device(*args):
        slab = args[2].shape[0]
        if mesh.shape["ind"] * BLK == 2 * slab and args[3].shape[1] % (2 * CW) == 0:
            return fused_call(*args)
        return general(*args)

    placed = (
        P(("snp", "ind"), None),
        P(("snp", "ind")),
        P(None, "ind"),
        P("ind", "snp"),
        P("ind", None),
        P("ind", None),
    )
    return jax.shard_map(
        per_device, mesh=mesh, in_specs=placed, out_specs=P("ind", "snp"), check_vma=False
    )
```

time: 182 us -> 50.5 us (0.28)
  the two profiles are of different devices: /device:TPU:9 before, /device:TPU:25 now
where the time goes in v1:
time: 50.5 us; the launch traced here: 50.4 us
  Pallas kernels  48.7 us (96%)
  local copies, waits for them, and re-layouts  1.67 us (3%)
    pallas_call x1, Pallas kernels, fused_call(): pl.pallas_call(functools.partial(fused, chips), out_shape=jax.ShapeDtypeS...  48.7 us
    unnamed x1, local copies, waits for them, and re-layouts  1.67 us

profile of v1, /device:TPU:25, one launch (start us, length us, event | category | flops | bytes accessed | tf_op | source)
XLA Modules:
  0.0 50.4 jit_solution(14724777089202545307)
XLA Ops:
  0.0 48.7 %shard_map.64 = bf16[256,512]{1,0:T(8,128)(2,1)} custom-call(s32[64,2048]{1,0:T(8,128)} %dos_h.1, f32[1,64]{1,0:T(1,128)} %bitcast.1, bf16[2048,1024]{1,0:T(8,128)(2,1)} %a_h.1, bf16[1024,512]{1,0:T(8,128)(2,1)} %b_h.1, bf16[256,512]{1,0:T(8,128)(2,1)} %d_h.1, bf16[256,2048]{1,0:T(8,128)(2,1)} %u_h.1), custom_call_target="tpu_custom_call" | custom-call | flops 2818572288 | bytes 8388608 | tf_op jit(solution)/shard_map/pallas_call | solution.py:255
  48.7 1.7 %copy.8 = bf16[256,512]{1,0:T(8,128)(2,1)} copy(bf16[256,512]{1,0:T(8,128)(2,1)} %shard_map.64) | data formatting | bytes 524288

commit v2 on v1

--- a/solution.py
+++ b/solution.py
@@ -8,6 +8,8 @@
 
 BLK = 512
 CW = 128
+PR = 256
+PARTS = BLK // PR
 BF = jnp.bfloat16
 F32 = jnp.float32
 
@@ -33,7 +35,7 @@
     last = chips - 1
 
     def block_at(j):
-        bottom = jnp.where(j < last - 1, j + 2, last - j)
+        bottom = jnp.where(j == 0, last, jnp.where(j == last, 0, j))
         return jnp.where(z == 0, bottom, lax.rem(z + 1 + j, chips))
 
     def load_a(j):
@@ -90,14 +92,21 @@
     def sib_copy(blk):
         return remote(sib_out.at[blk], sib_in.at[blk], sib_s.at[blk], sib_r.at[blk], sib)
 
-    def up_copy(blk, q):
-        return remote(up_out.at[blk, q], up_in.at[blk, q], up_s.at[blk, q], up_r.at[blk, q], me + 2)
-
-    def dn_copy(blk, q):
-        return remote(dn_out.at[blk, q], dn_in.at[blk, q], dn_s.at[blk, q], dn_r.at[blk, q], me - 2)
-
-    def w_copy(blk, q):
-        return remote(w.at[blk, q], w.at[blk, q], w_s.at[blk, q], w_r.at[blk, q], me + 2)
+    def piece(buf, blk, q, h):
+        return buf.at[blk, q, pl.ds(h * PR, PR)]
+
+    def line_copy(src, dst, ss, rs, blk, q, h, to):
+        return remote(piece(src, blk, q, h), piece(dst, blk, q, h),
+                      ss.at[blk, q * PARTS + h], rs.at[blk, q * PARTS + h], to)
+
+    def up_copy(blk, q, h):
+        return line_copy(up_out, up_in, up_s, up_r, blk, q, h, me + 2)
+
+    def dn_copy(blk, q, h):
+        return line_copy(dn_out, dn_in, dn_s, dn_r, blk, q, h, me - 2)
+
+    def w_copy(blk, q, h):
+        return line_copy(w, w, w_s, w_r, blk, q, h, me + 2)
 
     def out_copy(q):
         return remote(
@@ -124,14 +133,16 @@
             def _():
                 up_out[blk, q] = total.astype(BF)
 
-            @pl.when((z == 0) & (blk > (1 if q else 0)))
+            @pl.when((z == 0) & (blk > (last - 1 if q else 0)))
             def _():
-                up_copy(blk, q).start()
-
-            @pl.when((z == chips - 1) & (blk < chips - 1))
+                for h in range(PARTS):
+                    up_copy(blk, q, h).start()
+
+            @pl.when((z == last) & (blk < last))
             def _():
                 dn_out[blk, q] = total.astype(BF)
-                dn_copy(blk, q).start()
+                for h in range(PARTS):
+                    dn_copy(blk, q, h).start()
 
     load_b.wait()
 
@@ -162,23 +173,28 @@
             copy.start()
             sent.append(copy)
 
+        def relay(copy, out, arrived, blk, q):
+            for h in range(PARTS):
+                at = slice(h * PR, (h + 1) * PR)
+                copy(blk, q, h).wait_recv()
+                out[blk, q, at] = (acc[blk, q, at] + arrived[blk, q, at].astype(F32)).astype(BF)
+                send(copy(blk, q, h))
+
         def relay_up(blk, q):
-            up_copy(blk, q).wait_recv()
-            up_out[blk, q] = (acc[blk, q] + up_in[blk, q].astype(F32)).astype(BF)
-            send(up_copy(blk, q))
+            relay(up_copy, up_out, up_in, blk, q)
 
         def relay_dn(blk, q):
-            dn_copy(blk, q).wait_recv()
-            dn_out[blk, q] = (acc[blk, q] + dn_in[blk, q].astype(F32)).astype(BF)
-            send(dn_copy(blk, q))
+            relay(dn_copy, dn_out, dn_in, blk, q)
 
         def residual(q):
             total = acc[zz, q]
             if zz < last:
-                dn_copy(zz, q).wait_recv()
+                for h in range(PARTS):
+                    dn_copy(zz, q, h).wait_recv()
                 total = total + dn_in[zz, q].astype(F32)
             if zz > 0:
-                up_copy(zz, q).wait_recv()
+                for h in range(PARTS):
+                    up_copy(zz, q, h).wait_recv()
                 total = total + up_in[zz, q].astype(F32)
             acc[zz, q] = jnp.dot(dfull[...], total.astype(BF), preferred_element_type=F32)
 
@@ -193,39 +209,45 @@
                 ready.append(1)
 
         if 0 < zz < last:
-            pieces = [(last - zz + k, q, 0, k) for k in range(zz) for q in range(chunks)]
-            pieces += [(zz + k - 2, q, 1, k) for k in range(zz + 1, chips) for q in range(chunks)]
+            pieces = [(2 * k + last - zz + q + 0.5, q, 0, k) for k in range(zz) for q in range(chunks)]
+            pieces += [(zz + q, q, 1, last) for q in range(chunks)]
+            pieces += [(zz + 1 + k, 0, 1, k) for k in range(zz + 1, last)]
             for _, q, up, k in sorted(pieces):
                 (relay_up if up else relay_dn)(k, q)
         weights()
         for q in range(chunks):
+            if q:
+                for k in range(zz + 1, last):
+                    if zz > 0:
+                        relay_up(k, q)
             residual(q)
             for k in range(zz):
-                w_copy(k, q).wait_recv()
-                if zz < last:
-                    send(w_copy(k, q))
+                for h in range(PARTS):
+                    w_copy(k, q, h).wait_recv()
+                    if zz < last:
+                        send(w_copy(k, q, h))
                 acc[zz, q] = acc[zz, q] - jnp.dot(
                     ufull[:, k * BLK:(k + 1) * BLK], w[k, q], preferred_element_type=F32)
-            finish_chunk(zz, q, send)
+            w[zz, q] = acc[zz, q].astype(BF)
+            if zz < last:
+                for h in range(PARTS):
+                    send(w_copy(zz, q, h))
+            send(out_copy(q))
+            out_ref[:, pl.ds(pl.multiple_of(c * half + q * CW, CW), CW)] = w[zz, q, my_rows, :]
             if zz == 0 and q + 1 < chunks:
-                up_copy(1, q + 1).start()
+                for k in range(1, last):
+                    for h in range(PARTS):
+                        up_copy(k, q + 1, h).start()
         for copy in sent:
             copy.wait_send()
-        if zz == 0:
-            for k in range(1, chips):
-                for q in range(chunks):
-                    up_copy(k, q).wait_send()
-        if zz == last:
-            for k in range(last):
-                for q in range(chunks):
-                    dn_copy(k, q).wait_send()
-
-    def finish_chunk(zz, q, send):
-        w[zz, q] = acc[zz, q].astype(BF)
-        if zz < chips - 1:
-            send(w_copy(zz, q))
-        send(out_copy(q))
-        out_ref[:, pl.ds(pl.multiple_of(c * half + q * CW, CW), CW)] = w[zz, q, my_rows, :]
+        for q in range(chunks):
+            for h in range(PARTS):
+                if zz == 0:
+                    for k in range(1, chips):
+                        up_copy(k, q, h).wait_send()
+                if zz == last:
+                    for k in range(last):
+                        dn_copy(k, q, h).wait_send()
 
     for zz in range(chips):
         pl.when(z == zz)(functools.partial(role, zz))
@@ -273,9 +295,7 @@
             pltpu.VMEM(pieces, BF),
             pltpu.VMEM(pieces, BF),
             dma((4,)), dma((chips,)), dma((4,)), dma((chips,)), dma((chips,)),
-            dma((chips, chunks)), dma((chips, chunks)),
-            dma((chips, chunks)), dma((chips, chunks)),
-            dma((chips, chunks)), dma((chips, chunks)),
+            *[dma((chips, chunks * PARTS))] * 6,
             dma((chunks,)), dma((chunks,)),
         ],
         compiler_params=pltpu.CompilerParams(

time: 50.5 us -> 48.8 us (0.966)
  Pallas kernels: 48.7 us -> 47 us
    pallas_call x1, Pallas kernels: 48.7 us -> 47 us  [fused_call(): pl.pallas_call(functools.partial(fused, chips), out_shape=jax.ShapeDtypeS...]
where the time goes in v2:
time: 48.8 us; the launch traced here: 48.7 us
  Pallas kernels  47 us (96%)
  local copies, waits for them, and re-layouts  1.67 us (3%)
    pallas_call x1, Pallas kernels, fused_call(): pl.pallas_call(functools.partial(fused, chips), out_shape=jax.ShapeDtypeS...  47 us
    unnamed x1, local copies, waits for them, and re-layouts  1.67 us

profile of v2, /device:TPU:25, one launch (start us, length us, event | category | flops | bytes accessed | tf_op | source)
XLA Modules:
  0.0 48.7 jit_solution(13019576982404398578)
XLA Ops:
  0.0 47.0 %shard_map.64 = bf16[256,512]{1,0:T(8,128)(2,1)} custom-call(s32[64,2048]{1,0:T(8,128)} %dos_h.1, f32[1,64]{1,0:T(1,128)} %bitcast.1, bf16[2048,1024]{1,0:T(8,128)(2,1)} %a_h.1, bf16[1024,512]{1,0:T(8,128)(2,1)} %b_h.1, bf16[256,512]{1,0:T(8,128)(2,1)} %d_h.1, bf16[256,2048]{1,0:T(8,128)(2,1)} %u_h.1), custom_call_target="tpu_custom_call" | custom-call | flops 2818572288 | bytes 8388608 | tf_op jit(solution)/shard_map/pallas_call | solution.py:277
  47.0 1.7 %copy.8 = bf16[256,512]{1,0:T(8,128)(2,1)} copy(bf16[256,512]{1,0:T(8,128)(2,1)} %shard_map.64) | data formatting | bytes 524288

commit v3 on v2

--- a/solution.py
+++ b/solution.py
@@ -15,9 +15,9 @@
 
 
 def fused(chips, dos_h, freq_ref, a_h, b_h, d_h, u_h, out_ref,
-          dos, a, b, dfull, ufull, scaled, acc, sib_out, sib_in,
+          dos, a, b, dfull, ufull, placed, acc, sib_out, sib_in,
           up_out, up_in, dn_out, dn_in, w,
-          ld_sem, a_sem, x_sem, sib_s, sib_r, up_s, up_r, dn_s, dn_r, w_s, w_r, o_s, o_r):
+          ld_sem, a_sem, x_sem, sib_s, sib_r, up_s, up_r, dn_s, dn_r, w_s, w_r, o_s, o_r, l_s):
     me = lax.axis_index("ind")
     z, c = me // 2, me % 2
     sib = z * 2 + 1 - c
@@ -75,8 +75,13 @@
     eye = (lax.broadcasted_iota(jnp.int32, (snps, snps), 0)
            == lax.broadcasted_iota(jnp.int32, (snps, snps), 1))
     freq = jnp.sum(jnp.where(eye, jnp.broadcast_to(frow, (snps, snps)), 0.0), axis=1, keepdims=True)
-    scaled[...] = ((dos[...].astype(F32) - 2.0 * freq)
-                   * lax.rsqrt(2.0 * freq * (1.0 - freq))).astype(BF)
+    scaled = ((dos[...].astype(F32) - 2.0 * freq)
+              * lax.rsqrt(2.0 * freq * (1.0 - freq))).astype(BF)
+    my_side = me * snps // half
+    place = (lax.broadcasted_iota(jnp.int32, (snps, half), 1) + my_side * half
+             == lax.broadcasted_iota(jnp.int32, (snps, half), 0) + me * snps)
+    placed[...] = lax.dot_general(scaled, place.astype(F32).astype(BF), (((0,), (0,)), ((), ())),
+                                  preferred_element_type=F32).astype(BF)
 
     @pl.when((z == 0) | (z == chips - 1))
     def _():
@@ -114,13 +119,15 @@
             out_ref.at[:, pl.ds(pl.multiple_of(c * half + q * CW, CW), CW)],
             o_s.at[q], o_r.at[q], sib)
 
+    def own_copy(q):
+        return pltpu.make_async_copy(
+            w.at[z, q, my_rows],
+            out_ref.at[:, pl.ds(pl.multiple_of(c * half + q * CW, CW), CW)], l_s.at[q])
+
     def partial(blk, side):
         at = pl.ds(pl.multiple_of(blk * BLK, BLK), BLK)
         cols = pl.ds(pl.multiple_of(side * half, half), half)
-        place = (lax.broadcasted_iota(jnp.int32, (snps, half), 1) + side * half
-                 == lax.broadcasted_iota(jnp.int32, (snps, half), 0) + me * snps)
-        own = lax.dot_general(scaled[:, at], place.astype(F32).astype(BF),
-                              (((0,), (0,)), ((), ())), preferred_element_type=F32)
+        own = jnp.where(side == my_side, placed[at, :].astype(F32), 0.0)
         return own - jnp.dot(a[at, :], b[:, cols], preferred_element_type=F32)
 
     def finish(blk):
@@ -233,7 +240,7 @@
                 for h in range(PARTS):
                     send(w_copy(zz, q, h))
             send(out_copy(q))
-            out_ref[:, pl.ds(pl.multiple_of(c * half + q * CW, CW), CW)] = w[zz, q, my_rows, :]
+            own_copy(q).start()
             if zz == 0 and q + 1 < chunks:
                 for k in range(1, last):
                     for h in range(PARTS):
@@ -253,6 +260,7 @@
         pl.when(z == zz)(functools.partial(role, zz))
 
     for q in range(chunks):
+        own_copy(q).wait()
         out_copy(q).wait_recv()
     for k in range(chips):
         sib_copy(k).wait_send()
@@ -278,14 +286,14 @@
         functools.partial(fused, chips),
         out_shape=jax.ShapeDtypeStruct((rows, width), BF),
         in_specs=[hbm, vmem, hbm, hbm, hbm, hbm],
-        out_specs=vmem,
+        out_specs=hbm,
         scratch_shapes=[
             pltpu.VMEM((snps, slab), jnp.int32),
             pltpu.VMEM((slab, depth), BF),
             pltpu.VMEM((depth, width), BF),
             pltpu.VMEM((BLK, BLK), BF),
             pltpu.VMEM((BLK, slab - BLK), BF),
-            pltpu.VMEM((snps, slab), BF),
+            pltpu.VMEM((slab, half), BF),
             pltpu.VMEM(pieces, F32),
             pltpu.VMEM((chips, BLK, half), BF),
             pltpu.VMEM((chips, BLK, half), BF),
@@ -296,7 +304,7 @@
             pltpu.VMEM(pieces, BF),
             dma((4,)), dma((chips,)), dma((4,)), dma((chips,)), dma((chips,)),
             *[dma((chips, chunks * PARTS))] * 6,
-            dma((chunks,)), dma((chunks,)),
+            dma((chunks,)), dma((chunks,)), dma((chunks,)),
         ],
         compiler_params=pltpu.CompilerParams(
             collective_id=0, has_side_effects=True, vmem_limit_bytes=60 * 2**20),

time: 48.8 us -> 47 us (0.963)
  Pallas kernels: 47 us -> 45.2 us
    pallas_call x1, Pallas kernels: 47 us -> 45.2 us  [fused_call(): pl.pallas_call(functools.partial(fused, chips), out_shape=jax.ShapeDtypeS...]
where the time goes in v3:
time: 47 us; the launch traced here: 46.8 us
  Pallas kernels  45.2 us (96%)
  local copies, waits for them, and re-layouts  1.67 us (4%)
    pallas_call x1, Pallas kernels, fused_call(): pl.pallas_call(functools.partial(fused, chips), out_shape=jax.ShapeDtypeS...  45.2 us
    unnamed x1, local copies, waits for them, and re-layouts  1.67 us

profile of v3, /device:TPU:25, one launch (start us, length us, event | category | flops | bytes accessed | tf_op | source)
XLA Modules:
  0.0 46.8 jit_solution(3191188905469927595)
XLA Ops:
  0.0 45.2 %shard_map.64 = bf16[256,512]{1,0:T(8,128)(2,1)} custom-call(s32[64,2048]{1,0:T(8,128)} %dos_h.1, f32[1,64]{1,0:T(1,128)} %bitcast.1, bf16[2048,1024]{1,0:T(8,128)(2,1)} %a_h.1, bf16[1024,512]{1,0:T(8,128)(2,1)} %b_h.1, bf16[256,512]{1,0:T(8,128)(2,1)} %d_h.1, bf16[256,2048]{1,0:T(8,128)(2,1)} %u_h.1), custom_call_target="tpu_custom_call" | custom-call | flops 2818572288 | bytes 8388608 | tf_op jit(solution)/shard_map/pallas_call | solution.py:285
  45.2 1.7 %copy.8 = bf16[256,512]{1,0:T(8,128)(2,1)} copy(bf16[256,512]{1,0:T(8,128)(2,1)} %shard_map.64) | data formatting | bytes 524288

commit v4 on v3

--- a/solution.py
+++ b/solution.py
@@ -216,7 +216,7 @@
                 ready.append(1)
 
         if 0 < zz < last:
-            pieces = [(2 * k + last - zz + q + 0.5, q, 0, k) for k in range(zz) for q in range(chunks)]
+            pieces = [(2 * k + last - zz + q - 0.6, q, 0, k) for k in range(zz) for q in range(chunks)]
             pieces += [(zz + q, q, 1, last) for q in range(chunks)]
             pieces += [(zz + 1 + k, 0, 1, k) for k in range(zz + 1, last)]
             for _, q, up, k in sorted(pieces):

time: 47 us -> 46.2 us (0.983)
  Pallas kernels: 45.2 us -> 44.3 us
    pallas_call x1, Pallas kernels: 45.2 us -> 44.3 us  [fused_call(): pl.pallas_call(functools.partial(fused, chips), out_shape=jax.ShapeDtypeS...]
where the time goes in v4:
time: 46.2 us; the launch traced here: 46 us
  Pallas kernels  44.3 us (96%)
  local copies, waits for them, and re-layouts  1.67 us (4%)
    pallas_call x1, Pallas kernels, fused_call(): pl.pallas_call(functools.partial(fused, chips), out_shape=jax.ShapeDtypeS...  44.3 us
    unnamed x1, local copies, waits for them, and re-layouts  1.67 us

profile of v4, /device:TPU:25, one launch (start us, length us, event | category | flops | bytes accessed | tf_op | source)
XLA Modules:
  0.0 46.0 jit_solution(17075402619633135223)
XLA Ops:
  0.0 44.3 %shard_map.64 = bf16[256,512]{1,0:T(8,128)(2,1)} custom-call(s32[64,2048]{1,0:T(8,128)} %dos_h.1, f32[1,64]{1,0:T(1,128)} %bitcast.1, bf16[2048,1024]{1,0:T(8,128)(2,1)} %a_h.1, bf16[1024,512]{1,0:T(8,128)(2,1)} %b_h.1, bf16[256,512]{1,0:T(8,128)(2,1)} %d_h.1, bf16[256,2048]{1,0:T(8,128)(2,1)} %u_h.1), custom_call_target="tpu_custom_call" | custom-call | flops 2818572288 | bytes 8388608 | tf_op jit(solution)/shard_map/pallas_call | solution.py:285
  44.3 1.7 %copy.8 = bf16[256,512]{1,0:T(8,128)(2,1)} copy(bf16[256,512]{1,0:T(8,128)(2,1)} %shard_map.64) | data formatting | bytes 524288
